TPU v7x, 512 devices: a whole 4x8x8 slice. The times are simulated.
512 devices in a mesh: replica: 16 (over y, z_lo), fsdp: 32 (over x, z_hi, core).
Axes of the slice: x: 4, y: 8, z: 8 (z_hi: 4, z_lo: 2; z = z_hi * 2 + z_lo), core: 2. Of those that a mesh axis runs over, the one named last changes fastest.
Arguments:
- tokens: bfloat16 [16, 16384, 2048], P('replica', 'fsdp'), may hold values from -6 to 6
- key_cot: bfloat16 [16, 16384, 512], P('replica', 'fsdp'), may hold values from -6 to 6
- norm_gain: float32 [2048], replicated, may hold values from 0.25 to 1.75
- key_weight: float32 [16, 2048, 512], P('replica', 'fsdp'), may hold values from -0.125 to 0.125
- first_moment: float32 [16, 2048, 512], P('replica', 'fsdp'), may hold values from -60 to 60
- second_moment: float32 [16, 2048, 512], P('replica', 'fsdp'), may hold values from 10 to 1000
- inner_step: int32 [1], replicated, may hold values from 1 to 8
- global_prev: float32 [2048, 512], P('fsdp'), may hold values from -6 to 6
- outer_momentum: float32 [2048, 512], P('fsdp'), may hold values from -6 to 6
- replica_prev: float32 [16, 2048, 512], P('replica', 'fsdp'), may hold values from -6 to 6
Outputs:
- weight_new: float32 [16, 2048, 512], P('replica', 'fsdp')
- first_new: float32 [16, 2048, 512], P('replica', 'fsdp')
- second_new: float32 [16, 2048, 512], P('replica', 'fsdp')
- keys: bfloat16 [16, 16384, 512], P('replica', 'fsdp')
- blended: float32 [16, 2048, 512], P('replica', 'fsdp')
- momentum_new: float32 [2048, 512], P('fsdp')
Inputs may be any that keep to these rules, and one draw needn't show every extreme that they name: `inner_step`: the inner optimizer's step count, the same for every replica.
All inputs are finite; a program needn't handle non-finite values.
Results may differ from a plain program's by a relative error of at most 0.025.
Values may be sent and summed in bfloat16 or wider, within the bound.
A program may use at most 64 MiB of HBM per device.

v0:
```python
import jax
import jax.numpy as jnp
from jax import lax
from jax.sharding import PartitionSpec as P


def rms_normed(tokens, norm_gain):
    values = tokens.astype(jnp.float32)
    scale = lax.rsqrt(jnp.mean(values * values, axis=-1, keepdims=True) + 1e-05)
    return (values * scale * norm_gain).astype(jnp.bfloat16)


def adam_step(weight, first, second, grads, inner_step):
    count = inner_step[0].astype(jnp.float32)
    first_new = 0.9 * first + 0.1 * grads
    second_new = 0.95 * second + 0.05 * grads * grads
    first_hat = first_new / (1.0 - jnp.power(jnp.float32(0.9), count))
    second_hat = second_new / (1.0 - jnp.power(jnp.float32(0.95), count))
    change = 0.03 * (first_hat / (jnp.sqrt(second_hat) + 1e-08) + 0.1 * weight)
    return (change, first_new, second_new)


def grad_term(normed, cotangent):
    return lax.dot_general(
        normed, cotangent, (((0,), (0,)), ((), ())), preferred_element_type=jnp.float32
    )


def add_keys(normed, piece):
    return jnp.dot(normed, piece, preferred_element_type=jnp.float32)


def body(
    tokens,
    key_cot,
    norm_gain,
    key_weight,
    first_moment,
    second_moment,
    inner_step,
    global_prev,
    outer_momentum,
    replica_prev,
):
    normed = rms_normed(tokens[0], norm_gain)
    cotangent = key_cot[0]
    weight = key_weight[0]
    first_old = first_moment[0]
    second_old = second_moment[0]
    grads = lax.psum_scatter(
        grad_term(normed, cotangent).astype(jnp.bfloat16), "fsdp", scatter_dimension=0, tiled=True
    ).astype(jnp.float32)
    change, first_new, second_new = adam_step(weight, first_old, second_old, grads, inner_step)
    weight_new = weight - change
    projected = add_keys(
        normed, lax.all_gather(weight_new.astype(jnp.bfloat16), "fsdp", axis=0, tiled=True)
    )
    keys = projected.astype(jnp.bfloat16)
    snapshot = replica_prev[0]
    replicas = lax.axis_size("replica")
    drift = lax.psum(global_prev - snapshot, "replica")
    mean_drift = drift / replicas
    momentum_new = 0.9 * outer_momentum + mean_drift
    global_new = global_prev - 0.7 * (mean_drift + 0.9 * momentum_new)
    blended = 0.5 * global_new + 0.5 * snapshot
    return (
        weight_new[None],
        first_new[None],
        second_new[None],
        keys[None],
        blended[None],
        momentum_new,
    )


def solution(mesh):
    placed = (
        P("replica", "fsdp", None),
        P("replica", "fsdp", None),
        P(),
        P("replica", "fsdp", None),
        P("replica", "fsdp", None),
        P("replica", "fsdp", None),
        P(),
        P("fsdp", None),
        P("fsdp", None),
        P("replica", "fsdp", None),
    )
    return jax.shard_map(
        body,
        mesh=mesh,
        in_specs=placed,
        out_specs=(
            P("replica", "fsdp", None),
            P("replica", "fsdp", None),
            P("replica", "fsdp", None),
            P("replica", "fsdp", None),
            P("replica", "fsdp", None),
            P("fsdp", None),
        ),
        check_vma=False,
    )
```

profile of v0, /device:TPU:1, one launch (start us, length us, event | category | flops | bytes accessed | tf_op | source)
XLA Modules:
  0.0 193.1 jit_solution(12416950109230322182)
XLA Ops:
  8.0 0.0 copy-start
  8.0 0.0 copy-start.1
  8.0 0.0 reduce-scatter.2.cloned.1.call-start
  8.1 2.2 %fusion.2 = f32[512]{0:T(512)S(1)} fusion(bf16[1,512,2048]{2,1,0:T(8,128)(2,1)} %param.10), kind=kLoop, calls=%fused_computation.4 | loop fusion | flops 3145216 | bytes 2099200 | tf_op jit(solution)/shard_map/reduce_sum | solution.py:9
  10.3 0.0 copy-done
  10.3 0.1 copy-done.1
  10.4 3.4 %convolution_convert_fusion = bf16[2048,512]{1,0:T(8,128)(2,1)} fusion(bf16[1,512,2048]{2,1,0:T(8,128)(2,1)S(1)} %copy-done.1, f32[2048]{0:T(1024)} %param.12, f32[512]{0:T(512)S(1)} %add_rsqrt_fusion, bf16[1,512,512]{2,1,0:T(8,128)(2,1)S(1)} %copy-done), kind=kOutput, calls=%fused_computation.9 | convolution fusion | flops 1078984704 | bytes 4728832 | tf_op jit(solution)/shard_map/dot_general | solution.py:24
  13.8 0.0 copy-start.2
  13.9 0.0 copy-start.3
  13.9 0.0 copy-start.4
  13.9 0.0 copy-start.5
  13.9 0.0 copy-start.6
  13.9 0.0 copy-start.7
  13.9 0.0 copy-start.8
  13.9 0.0 reduce-scatter.2.cloned.1.call-update
  13.9 0.0 all-reduce.2.cloned.1.call-start
  14.0 0.8 copy-done.2
  14.8 0.1 copy-done.3
  14.8 0.7 bitcast_subtract_fusion
  15.5 0.0 all-reduce.2.cloned.1.call-update
  15.5 0.0 all-gather.2.cloned.1.call-start
  16.3 102.4 %reduce-scatter.2.cloned.1.call-done = bf16[64,512]{1,0:T(8,128)(2,1)} async-done(((bf16[2048,512]{1,0:T(8,128)(2,1)}), bf16[64,512]{1,0:T(8,128)(2,1)}) %reduce-scatter.2.cloned.1.call-update) | async-done | bytes 65552 | tf_op jit(solution)/shard_map/reduce_scatter | solution.py:50
  118.7 0.0 copy-done.4
  118.7 0.0 copy-done.5
  118.7 0.0 copy-done.6
  118.7 1.7 fusion.30
  120.4 0.0 all-gather.2.cloned.1.call-update
  120.4 32.3 %all-reduce.2.cloned.1.call-done = f32[64,512]{1,0:T(8,128)} async-done(((f32[64,512]{1,0:T(8,128)}), f32[64,512]{1,0:T(8,128)}) %all-reduce.2.cloned.1.call-update) | async-done | bytes 131088 | tf_op jit(solution)/shard_map/psum | solution.py:61
  152.8 0.0 copy-done.7
  152.8 1.7 fusion.25
  154.4 27.6 %all-gather.2.cloned.1.call-done = bf16[2048,512]{1,0:T(8,128)(2,1)} async-done(((bf16[64,512]{1,0:T(8,128)(2,1)}), bf16[2048,512]{1,0:T(8,128)(2,1)}) %all-gather.2.cloned.1.call-update) | async-done | bytes 2097168 | tf_op jit(solution)/shard_map/all_gather | solution.py:56
  182.0 0.0 copy-done.8
  182.0 3.7 %fusion.18 = bf16[1,512,512]{2,1,0:T(8,128)(2,1)} fusion(bf16[2048,512]{1,0:T(8,128)(2,1)} %all-gather.2.cloned.1.call-done, bf16[1,512,2048]{2,1,0:T(8,128)(2,1)S(1)} %copy-done.1, f32[2048]{0:T(1024)S(1)} %copy-done.8, f32[512]{0:T(512)S(1)} %add_rsqrt_fusion), kind=kOutput, calls=%fused_computation.17 | convolution fusion | flops 1078198272 | bytes 4728832 | tf_op jit(solution)/shard_map/dot_general | solution.py:30
  (1 shorter events, 0.0 us)
Async XLA Ops:
  8.0 2.3 %copy-start = (bf16[1,512,512]{2,1,0:T(8,128)(2,1)S(1)}, bf16[1,512,512]{2,1,0:T(8,128)(2,1)}, u32[]{:S(2)}) copy-start(bf16[1,512,512]{2,1,0:T(8,128)(2,1)} %param.11) | copy-start | bytes 1572868
  8.0 2.4 %copy-start.1 = (bf16[1,512,2048]{2,1,0:T(8,128)(2,1)S(1)}, bf16[1,512,2048]{2,1,0:T(8,128)(2,1)}, u32[]{:S(2)}) copy-start(bf16[1,512,2048]{2,1,0:T(8,128)(2,1)} %param.10) | copy-start | bytes 6291460
  8.0 110.7 %reduce-scatter.2.cloned.1.call-start = ((), (), s32[]{:S(2)}) async-start(), calls=%async_computation.1 | async-start | bytes 2162688 | tf_op jit(solution)/shard_map/reduce_scatter | solution.py:50
  13.8 0.9 copy-start.2
  13.9 1.0 copy-start.3
  13.9 104.9 %copy-start.4 = (f32[1,64,512]{2,1,0:T(8,128)S(1)}, f32[1,64,512]{2,1,0:T(8,128)}, u32[]{:S(2)}) copy-start(f32[1,64,512]{2,1,0:T(8,128)} %param.15) | copy-start | bytes 393220
  13.9 104.9 %copy-start.5 = (f32[1,64,512]{2,1,0:T(8,128)S(1)}, f32[1,64,512]{2,1,0:T(8,128)}, u32[]{:S(2)}) copy-start(f32[1,64,512]{2,1,0:T(8,128)} %param.14) | copy-start | bytes 393220
  13.9 104.9 %copy-start.6 = (f32[1,64,512]{2,1,0:T(8,128)S(1)}, f32[1,64,512]{2,1,0:T(8,128)}, u32[]{:S(2)}) copy-start(f32[1,64,512]{2,1,0:T(8,128)} %param.13) | copy-start | bytes 393220
  13.9 138.9 %copy-start.7 = (f32[64,512]{1,0:T(8,128)S(1)}, f32[64,512]{1,0:T(8,128)}, u32[]{:S(2)}) copy-start(f32[64,512]{1,0:T(8,128)} %param.18) | copy-start | bytes 393220
  13.9 168.1 %copy-start.8 = (f32[2048]{0:T(1024)S(1)}, f32[2048]{0:T(1024)}, u32[]{:S(2)}) copy-start(f32[2048]{0:T(1024)} %param.12) | copy-start | bytes 24580
  13.9 138.8 %all-reduce.2.cloned.1.call-start = ((), (), s32[]{:S(2)}) async-start(), calls=%async_computation.3 | async-start | bytes 262144 | tf_op jit(solution)/shard_map/psum | solution.py:61
  15.5 166.5 %all-gather.2.cloned.1.call-start = ((), (), s32[]{:S(2)}) async-start(), calls=%async_computation.2 | async-start | bytes 2162688 | tf_op jit(solution)/shard_map/all_gather | solution.py:56
Sparse Core Ops, SparseCore 0:
  14.0 104.6 reduce-scatter.1
  122.4 59.5 all-gather.1
Sparse Core Ops, SparseCore 1:
  17.9 134.8 all-reduce.1
where the time goes:
time: 193 us
  waiting for transfers between devices  162 us (84%)
  between operations  16.3 us (8%)
  matrix products  7.13 us (4%)
  other arithmetic  6.26 us (3%)
    reduce_scatter x1, waiting for transfers between devices, body(): lax.psum_scatter(grad_term(normed, cotangent).astype(jnp.bfloat16), 'fsdp...  102 us
    psum x1, waiting for transfers between devices, body(): drift = lax.psum(global_prev - snapshot, 'replica')  32.3 us
    all_gather x1, waiting for transfers between devices, body(): lax.all_gather(weight_new.astype(jnp.bfloat16), 'fsdp', axis=0, tiled=True)  27.6 us
  transfers between devices with their start and end apart: 3, of which 3 were waited for; matrix products, arithmetic and copies ran while one was open for 2% of the time, Pallas kernels for 0%

commit v1 on v0

v1 whole, which is shorter than its diff:
```python
import math

import jax
import jax.numpy as jnp
from jax import lax
from jax.experimental import pallas as pl
from jax.experimental.pallas import tpu as pltpu
from jax.sharding import PartitionSpec as P

F32, BF16 = jnp.float32, jnp.bfloat16
MESH = pl.DeviceIdType.MESH
TOK, D, KW, ROWS, WIDE = 512, 2048, 512, 64, 256
CONTRACT_FIRST = (((0,), (0,)), ((), ()))

CHUNKS = (
    (1, 32, 16, "z", 0),
    (1, 48, 16, "z", 1),
    (1, 0, 16, "x", 0),
    (1, 16, 16, "x", 1),
    (0, 0, 32, "x", 0),
    (0, 32, 32, "x", 1),
)
HALVES = (1, 0)
N_SEMS = 17


def pair_bit(kind, p):
    return ((p + 1) // 2) % 2 if kind == 0 else p // 2


def pair_of(kind, p):
    return p + 1 - 2 * (p % 2) if kind == 0 else 3 - p


class Place:
    def __init__(self):
        f, r = lax.axis_index("fsdp"), lax.axis_index("replica")
        self.x, self.z, self.c = f // 8, (f // 2) % 4, f % 2
        self.y, self.l = r // 2, r % 2

    def at(self, **other):
        v = {**vars(self), **other}
        return (v["y"] * 2 + v["l"], (v["x"] * 4 + v["z"]) * 2 + v["c"])

    def partners(self):
        for o in (1, 2, 3):
            yield self.at(x=(self.x + o) % 4)
            yield self.at(z=(self.z + o) % 4)
        yield self.at(c=1 - self.c)
        for step in range(4):
            yield self.drift_partner(step)

    def drift_partner(self, step):
        y = self.y
        if step == 0:
            return self.at(y=y + 1 - 2 * (y % 2))
        if step == 1:
            return self.at(y=y + 2 - 4 * ((y // 2) % 2))
        if step == 2:
            return self.at(y=(y + 4) % 8)
        return self.at(l=1 - self.l)


def up(ref_value):
    return ref_value.astype(F32)


def chunk_steps(here, chunk, bufs, sems, w_ref, adam):
    half, row0, nr, axis, first = chunk
    g, rc, s1, r1, s2, r2, sq, rq = bufs
    send_sem, recv_sem = sems
    other_axis = "z" if axis == "x" else "x"
    p, q, c = getattr(here, axis), getattr(here, other_axis), here.c
    k1, k2 = first, 1 - first
    b1, b2 = pair_bit(k1, p), pair_bit(k2, p)
    p1, p2 = pair_of(k1, p), pair_of(k2, p)
    to1, to2 = here.at(**{axis: p1}), here.at(**{axis: p2})
    sibling = here.at(c=1 - c)
    started = []

    def copy(n, src, dst, to):
        return pltpu.make_async_remote_copy(
            src_ref=src,
            dst_ref=dst,
            send_sem=send_sem.at[n],
            recv_sem=recv_sem.at[n],
            device_id=to,
            device_id_type=MESH,
        )

    def send(*what):
        one = copy(*what)
        one.start()
        started.append(one)
        return one

    def drain(keep):
        while len(started) > keep:
            started.pop(0).wait_send()

    c_out = send(0, g.at[1 - c, 1 - b1], rc.at[1 - b1], sibling)
    c_in = send(1, g.at[1 - c, b1], rc.at[b1], sibling)
    yield
    c_out.wait_recv()
    for part, n in ((1 - b2, 2), (b2, 3)):
        s1[part] = (up(g[c, 1 - b1, part]) + up(rc[1 - b1, part])).astype(BF16)
        if n == 2:
            first_in = send(2, s1.at[part], r1.at[part], to1)
        else:
            second_in = send(3, s1.at[part], r1.at[part], to1)
    yield
    c_in.wait_recv()
    first_in.wait_recv()
    s2[...] = (up(g[c, b1, 1 - b2]) + up(rc[b1, 1 - b2]) + up(r1[1 - b2])).astype(BF16)
    pair_in = send(4, s2, r2, to2)
    yield
    second_in.wait_recv()
    drain(1)
    pair_in.wait_recv()
    sq[...] = (up(g[c, b1, b2]) + up(rc[b1, b2]) + up(r1[b2]) + up(r2[...])).astype(BF16)
    direct = []
    for o in (2, 1, 3):
        to = (q + o) % 4
        direct.append(send(4 + o, sq.at[to], rq.at[o - 1], here.at(**{other_axis: to})))
    yield
    drain(3)
    for one in direct:
        one.wait_recv()
    total = up(sq[q]) + up(rq[0]) + up(rq[1]) + up(rq[2])
    w_own = adam(half, row0, nr, total)

    def piece(pp, qq, cc):
        x, z = (pp, qq) if axis == "x" else (qq, pp)
        return w_ref.at[half, x, z, cc, pl.ds(row0, nr)]

    def group(pp, cc):
        if axis == "x":
            return w_ref.at[half, pp, :, cc, pl.ds(row0, nr)]
        return w_ref.at[half, :, pp, cc, pl.ds(row0, nr)]

    mine = piece(p, q, c)
    mine[...] = w_own
    direct = []
    for o in (2, 1, 3):
        direct.append(send(7 + o, mine, mine, here.at(**{other_axis: (q + o) % 4})))
    yield
    drain(3)
    for one in direct:
        one.wait_recv()
    own = group(p, c)
    in2 = send(11, own, own, to2)
    in1 = send(12, own, own, to1)
    cs = [send(13, own, own, sibling)]
    yield
    drain(3)
    in2.wait_recv()
    own = group(p2, c)
    in12 = send(14, own, own, to1)
    cs.append(send(15, own, own, sibling))
    yield
    drain(2)
    in1.wait_recv()
    own = group(p1, c)
    cs.append(send(16, own, own, sibling))
    yield
    in12.wait_recv()
    own = group(pair_of(k2, p1), c)
    cs.append(send(17, own, own, sibling))
    yield
    for one in cs:
        one.wait_recv()
    yield
    drain(0)
    yield


def kernel(
    tokens, key_cot, gain, key_weight, first_moment, second_moment, inner_step, global_prev, outer_momentum, replica_prev,
    weight_out, first_out, second_out, keys_out, blended_out, momentum_out,
    tok, cot, cs, scale, kw, m1, m2, gp, om, rp, gcol, wn, fn, sn, bl, mn, keys, w_all, ds, dr,
    in_sem, out_sem, d_send, d_recv, *chunk_scratch,
):
    here = Place()
    c = here.c

    def load(src, dst, n):
        one = pltpu.make_async_copy(src, dst, in_sem.at[n])
        one.start()
        return one

    quarter = TOK // 4
    tok_in = [load(tokens.at[0, pl.ds(i * quarter, quarter)], tok.at[pl.ds(i * quarter, quarter)], i) for i in range(4)]
    cot_in = load(key_cot.at[0], cot, 4)
    rest = [
        load(key_weight.at[0], kw, 5),
        load(first_moment.at[0], m1, 6),
        load(second_moment.at[0], m2, 7),
        load(global_prev, gp, 8),
        load(outer_momentum, om, 9),
    ]
    rp_in = load(replica_prev.at[0], rp, 10)

    barrier = pltpu.get_barrier_semaphore()
    n_partners = 0
    for to in here.partners():
        pl.semaphore_signal(barrier, inc=1, device_id=to, device_id_type=MESH)
        n_partners += 1

    for i in range(4):
        tok_in[i].wait()
        if i == 0:
            cot_in.wait()
        rows = slice(i * quarter, (i + 1) * quarter)
        v = up(tok[rows, :])
        s = lax.rsqrt(jnp.sum(v * v, axis=1, keepdims=True) * (1.0 / D) + 1e-05)
        scale[rows, :] = s
        cs[rows, :] = (up(cot[rows, :]) * s).astype(BF16)

    def gemm1(half):
        for x in range(4):
            part = lax.dot_general(
                tok[:, x * 512 : (x + 1) * 512],
                cs[:, half * WIDE : (half + 1) * WIDE],
                CONTRACT_FIRST,
                preferred_element_type=F32,
            ).astype(BF16)
            for i, (h, row0, nr, axis, first) in enumerate(CHUNKS):
                if h != half:
                    continue
                g = chunk_scratch[10 * i]
                for z in range(4):
                    p, q = (x, z) if axis == "x" else (z, x)
                    b1, b2 = pair_bit(first, p), pair_bit(1 - first, p)
                    for cc in range(2):
                        at = (z * 2 + cc) * ROWS + row0
                        g[cc, b1, b2, q] = part[at : at + nr]

    def adam(half, row0, nr, total):
        rows, cols = slice(row0, row0 + nr), slice(half * WIDE, (half + 1) * WIDE)
        count = jnp.full((1, WIDE), inner_step[0], jnp.int32).astype(F32)
        gains = gcol[rows, :]
        grads = total * gains
        first_new = 0.9 * m1[rows, cols] + 0.1 * grads
        second_new = 0.95 * m2[rows, cols] + 0.05 * grads * grads
        first_hat = first_new / (1.0 - jnp.exp(count * math.log(0.9)))
        second_hat = second_new / (1.0 - jnp.exp(count * math.log(0.95)))
        weight = kw[rows, cols]
        change = 0.03 * (first_hat / (jnp.sqrt(second_hat) + 1e-08) + 0.1 * weight)
        weight_new = weight - change
        fn[rows, cols] = first_new
        sn[rows, cols] = second_new
        wn[rows, cols] = weight_new
        return (weight_new * gains).astype(BF16)

    outs = []

    def store(src, dst):
        one = pltpu.make_async_copy(src, dst, out_sem.at[len(outs)])
        one.start()
        outs.append(one)

    def drift_steps():
        rp_in.wait()
        ds[0] = rp[...].astype(BF16)
        for step in range(4):
            one = pltpu.make_async_remote_copy(
                src_ref=ds.at[step],
                dst_ref=dr.at[step],
                send_sem=d_send.at[step],
                recv_sem=d_recv.at[step],
                device_id=here.drift_partner(step),
                device_id_type=MESH,
            )
            one.start()
            yield
            one.wait()
            total = up(ds[step]) + up(dr[step])
            if step < 3:
                ds[step + 1] = total.astype(BF16)
        mean_drift = gp[...] - total * (1.0 / 16)
        momentum_new = 0.9 * om[...] + mean_drift
        global_new = gp[...] - 0.7 * (mean_drift + 0.9 * momentum_new)
        mn[...] = momentum_new
        bl[...] = 0.5 * global_new + 0.5 * rp[...]
        store(mn, momentum_out)
        store(bl, blended_out.at[0])
        yield

    def gemm2(half):
        w = w_all[half].reshape(D, WIDE)
        cols = slice(half * WIDE, (half + 1) * WIDE)
        part = jnp.dot(tok[...], w, preferred_element_type=F32)
        keys[half] = (part * scale[...]).astype(BF16)
        store(keys.at[half], keys_out.at[0, :, pl.ds(half * WIDE, WIDE)])

    chunks = [
        chunk_steps(here, chunk, chunk_scratch[10 * i : 10 * i + 8], chunk_scratch[10 * i + 8 : 10 * i + 10], w_all, adam)
        for i, chunk in enumerate(CHUNKS)
    ]
    drift = drift_steps()

    gemm1(HALVES[0])
    pl.semaphore_wait(barrier, n_partners)
    for i, chunk in enumerate(CHUNKS):
        if chunk[0] == HALVES[0]:
            next(chunks[i])
    next(drift)
    gemm1(HALVES[1])
    for i, chunk in enumerate(CHUNKS):
        if chunk[0] == HALVES[1]:
            next(chunks[i])
    for one in rest:
        one.wait()
    lane = lax.broadcasted_iota(jnp.int32, (ROWS, 128), 1)
    row = lax.broadcasted_iota(jnp.int32, (ROWS, 128), 0)
    gains = gain[pl.ds(here.x * 4 + here.z, 1), :]
    picked = jnp.where(lane == row + ROWS * c, jnp.broadcast_to(gains, (ROWS, 128)), 0.0)
    gcol[...] = jnp.broadcast_to(jnp.sum(picked, axis=1, keepdims=True), (ROWS, WIDE))

    for level in range(1, 9):
        for one in chunks:
            next(one)
        if level == 4:
            store(wn, weight_out.at[0])
            store(fn, first_out.at[0])
            store(sn, second_out.at[0])
        if 2 <= level <= 5:
            next(drift)
    for half in HALVES:
        for i, chunk in enumerate(CHUNKS):
            if chunk[0] == half:
                next(chunks[i])
        gemm2(half)
    for one in chunks:
        next(one)
    for one in outs:
        one.wait()


def chunk_scratch(nr):
    return [
        pltpu.VMEM((2, 2, 2, 4, nr, WIDE), BF16),
        pltpu.VMEM((2, 2, 4, nr, WIDE), BF16),
        pltpu.VMEM((2, 4, nr, WIDE), BF16),
        pltpu.VMEM((2, 4, nr, WIDE), BF16),
        pltpu.VMEM((4, nr, WIDE), BF16),
        pltpu.VMEM((4, nr, WIDE), BF16),
        pltpu.VMEM((4, nr, WIDE), BF16),
        pltpu.VMEM((3, nr, WIDE), BF16),
        pltpu.SemaphoreType.DMA((18,)),
        pltpu.SemaphoreType.DMA((18,)),
    ]


def body(tokens, key_cot, norm_gain, key_weight, first_moment, second_moment, inner_step, global_prev, outer_momentum, replica_prev):
    anywhere = pl.BlockSpec(memory_space=pl.ANY)
    small = jax.ShapeDtypeStruct((1, ROWS, KW), F32)
    shard = pltpu.VMEM((ROWS, KW), F32)
    scratch = [
        pltpu.VMEM((TOK, D), BF16),
        pltpu.VMEM((TOK, KW), BF16),
        pltpu.VMEM((TOK, KW), BF16),
        pltpu.VMEM((TOK, 1), F32),
        *[shard] * 6,
        pltpu.VMEM((ROWS, WIDE), F32),
        *[shard] * 5,
        pltpu.VMEM((2, TOK, WIDE), BF16),
        pltpu.VMEM((2, 4, 4, 2, ROWS, WIDE), BF16),
        pltpu.VMEM((4, ROWS, KW), BF16),
        pltpu.VMEM((4, ROWS, KW), BF16),
        pltpu.SemaphoreType.DMA((11,)),
        pltpu.SemaphoreType.DMA((7,)),
        pltpu.SemaphoreType.DMA((4,)),
        pltpu.SemaphoreType.DMA((4,)),
    ]
    for chunk in CHUNKS:
        scratch += chunk_scratch(chunk[2])
    return pl.pallas_call(
        kernel,
        out_shape=(
            small,
            small,
            small,
            jax.ShapeDtypeStruct((1, TOK, KW), BF16),
            small,
            jax.ShapeDtypeStruct((ROWS, KW), F32),
        ),
        in_specs=[
            anywhere,
            anywhere,
            pl.BlockSpec(memory_space=pltpu.VMEM),
            anywhere,
            anywhere,
            anywhere,
            pl.BlockSpec(memory_space=pltpu.SMEM),
            anywhere,
            anywhere,
            anywhere,
        ],
        out_specs=(anywhere,) * 6,
        scratch_shapes=scratch,
        name="step",
        compiler_params=pltpu.CompilerParams(
            collective_id=0, has_side_effects=True, vmem_limit_bytes=56 * 2**20
        ),
    )(
        tokens, key_cot, norm_gain.reshape(16, 128), key_weight, first_moment, second_moment, inner_step,
        global_prev, outer_momentum, replica_prev,
    )


def solution(mesh):
    split = P("replica", "fsdp", None)
    rows = P("fsdp", None)
    return jax.shard_map(
        body,
        mesh=mesh,
        in_specs=(split, split, P(), split, split, split, P(), rows, rows, split),
        out_specs=(split, split, split, split, split, rows),
        check_vma=False,
    )
```

time: 193 us -> 61.7 us (0.32)
  waiting for transfers between devices: 162 us -> 0 us
  Pallas kernels: 0 us -> 51.3 us
  between operations: 16.3 us -> 1.3 us
  local copies, waits for them, and re-layouts: 0.98 us -> 8.83 us
  matrix products: 7.13 us -> 0 us
  other arithmetic: 6.26 us -> 0 us
    reduce_scatter x1 -> x0, waiting for transfers between devices: 102 us -> none  [body(): lax.psum_scatter(grad_term(normed, cotangent).astype(jnp.bfloat16), 'fsdp...]
    pallas_call x0 -> x1, Pallas kernels: none -> 51.3 us  [body(): pl.pallas_call(kernel, out_shape=(small, small, small, jax.ShapeDtypeStru...]
    psum x1 -> x0, waiting for transfers between devices: 32.3 us -> none  [body(): drift = lax.psum(global_prev - snapshot, 'replica')]
    all_gather x1 -> x0, waiting for transfers between devices: 27.6 us -> none  [body(): lax.all_gather(weight_new.astype(jnp.bfloat16), 'fsdp', axis=0, tiled=True)]
    unnamed x18 -> x8, local copies, waits for them, and re-layouts: 0.98 us -> 8.83 us
    dot_general x2 -> x0, matrix products: 7.13 us -> none  [the longest x1 3.69 us: add_keys(): return jnp.dot(normed, piece, preferred_element_type=jnp.float32)]
    reduce_sum x1 -> x0, other arithmetic: 2.23 us -> none  [rms_normed(): scale = lax.rsqrt(jnp.mean(values * values, axis=-1, keepdims=True) + 1e-05)]
  transfers between devices with their start and end apart: 3 -> 0, of which waited for: 3 -> 0; matrix products, arithmetic and copies ran while one was open for 2% -> 0% of each run, Pallas kernels for 0% -> 0%
where the time goes in v1:
time: 61.7 us; the launch traced here: 61.4 us
  Pallas kernels  51.3 us (83%)
  local copies, waits for them, and re-layouts  8.83 us (14%)
  between operations  1.3 us (2%)
    pallas_call x1, Pallas kernels, body(): pl.pallas_call(kernel, out_shape=(small, small, small, jax.ShapeDtypeStru...  51.3 us
    unnamed x8, local copies, waits for them, and re-layouts  8.83 us

profile of v1, /device:TPU:1, one launch (start us, length us, event | category | flops | bytes accessed | tf_op | source)
XLA Modules:
  0.0 61.4 jit_solution(17073416460637365320)
XLA Ops:
  1.3 51.3 %step.1 = (f32[1,64,512]{2,1,0:T(8,128)}, f32[1,64,512]{2,1,0:T(8,128)}, f32[1,64,512]{2,1,0:T(8,128)}, bf16[1,512,512]{2,1,0:T(8,128)(2,1)}, f32[1,64,512]{2,1,0:T(8,128)}, /*index=5*/f32[64,512]{1,0:T(8,128)}) custom-call(bf16[1,512,2048]{2,1,0:T(8,128)(2,1)} %tokens.1, bf16[1,512,512]{2,1,0:T(8,128)(2,1)} %key_cot.1, f32[16,128]{1,0:T(8,128)} %bitcast.1, ...), custom_call_target="tpu_custom_call" | custom-call | tf_op jit(solution)/shard_map/step/pallas_call | solution.py:378
  52.6 0.0 copy-start
  52.6 1.6 %copy.23 = f32[1,64,512]{2,1,0:T(8,128)} copy(f32[1,64,512]{2,1,0:T(8,128)} %get-tuple-element.12) | data formatting | bytes 262144
  54.2 1.6 %copy.24 = f32[1,64,512]{2,1,0:T(8,128)} copy(f32[1,64,512]{2,1,0:T(8,128)} %get-tuple-element.13) | data formatting | bytes 262144
  55.8 1.6 %copy.25 = f32[1,64,512]{2,1,0:T(8,128)} copy(f32[1,64,512]{2,1,0:T(8,128)} %get-tuple-element.14) | data formatting | bytes 262144
  57.3 1.9 %copy.26 = bf16[1,512,512]{2,1,0:T(8,128)(2,1)} copy(bf16[1,512,512]{2,1,0:T(8,128)(2,1)} %get-tuple-element.15) | data formatting | bytes 1048576
  59.2 1.6 %copy.27 = f32[1,64,512]{2,1,0:T(8,128)} copy(f32[1,64,512]{2,1,0:T(8,128)} %get-tuple-element.16) | data formatting | bytes 262144
  60.8 0.0 copy-done
  60.8 0.7 %copy.28 = f32[64,512]{1,0:T(8,128)} copy(f32[64,512]{1,0:T(8,128)S(1)} %copy-done) | data formatting | bytes 262144
Async XLA Ops:
  52.6 8.2 %copy-start = (f32[64,512]{1,0:T(8,128)S(1)}, f32[64,512]{1,0:T(8,128)}, u32[]{:S(2)}) copy-start(f32[64,512]{1,0:T(8,128)} %get-tuple-element.17) | copy-start | bytes 393220

commit v2 on v1

v2 whole, which is shorter than its diff:
```python
import math

import jax
import jax.numpy as jnp
from jax import lax
from jax.experimental import pallas as pl
from jax.experimental.pallas import tpu as pltpu
from jax.sharding import PartitionSpec as P

F32, BF16 = jnp.float32, jnp.bfloat16
MESH = pl.DeviceIdType.MESH
TOK, D, KW, ROWS, WIDE = 512, 2048, 512, 64, 256
CONTRACT_FIRST = (((0,), (0,)), ((), ()))

CHUNKS = (
    (1, 32, 32, "z"),
    (1, 0, 32, "x"),
    (0, 0, 32, "x"),
    (0, 32, 32, "x"),
)
HALVES = (1, 0)
OFFSETS = (2, 1, 3)


class Place:
    def __init__(self):
        f, r = lax.axis_index("fsdp"), lax.axis_index("replica")
        self.x, self.z, self.c = f // 8, (f // 2) % 4, f % 2
        self.y, self.l = r // 2, r % 2

    def at(self, **other):
        v = {**vars(self), **other}
        return (v["y"] * 2 + v["l"], (v["x"] * 4 + v["z"]) * 2 + v["c"])

    def partners(self):
        for o in OFFSETS:
            yield self.at(z=(self.z + o) % 4)
        for o in OFFSETS:
            yield self.at(x=(self.x + o) % 4)
        yield self.at(c=1 - self.c)
        yield self.at(l=1 - self.l)
        yield self.at(y=(self.y + 1) % 8)
        yield self.at(y=(self.y + 7) % 8)


def up(ref_value):
    return ref_value.astype(F32)


def remote(src, dst, send_sem, recv_sem, to):
    return pltpu.make_async_remote_copy(
        src_ref=src,
        dst_ref=dst,
        send_sem=send_sem,
        recv_sem=recv_sem,
        device_id=to,
        device_id_type=MESH,
    )


def chunk_steps(here, chunk, bufs, sems, w_ref, adam):
    half, row0, nr, axis = chunk
    g, rc, s1, r1, sq, rq = bufs
    send_sem, recv_sem = sems
    other_axis = "z" if axis == "x" else "x"
    p, q, c = getattr(here, axis), getattr(here, other_axis), here.c
    sibling = here.at(c=1 - c)

    def along_p(o):
        return here.at(**{axis: (p + o) % 4})

    def along_q(o):
        return here.at(**{other_axis: (q + o) % 4})

    def send(n, src, dst, to, m=None):
        one = remote(src, dst, send_sem.at[n], recv_sem.at[n if m is None else m], to)
        one.start()
        return one

    def all_of(n, ref):
        return remote(ref, ref, send_sem.at[n], recv_sem.at[n], sibling)

    swap = send(0, g.at[1 - c], rc, sibling)
    yield
    swap.wait_recv()
    for o in OFFSETS:
        to = (p + o) % 4
        s1[to] = (up(g[c, to]) + up(rc[to])).astype(BF16)
        send(1, s1.at[to], r1.at[o - 1], along_p(o))
    yield
    mine = up(g[c, p]) + up(rc[p])
    all_of(1, r1).wait_recv()
    sq[...] = (mine + up(r1[0]) + up(r1[1]) + up(r1[2])).astype(BF16)
    for o in OFFSETS:
        send(2, sq.at[(q + o) % 4], rq.at[o - 1], along_q(o))
    yield
    swap.wait_send()
    all_of(2, rq).wait_recv()
    w_own = adam(half, row0, nr, up(sq[q]) + up(rq[0]) + up(rq[1]) + up(rq[2]))

    def piece(pp, qq, cc):
        x, z = (pp, qq) if axis == "x" else (qq, pp)
        return w_ref.at[half, x, z, cc, pl.ds(row0, nr)]

    def group(pp, cc):
        if axis == "x":
            return w_ref.at[half, pp, :, cc, pl.ds(row0, nr)]
        return w_ref.at[half, :, pp, cc, pl.ds(row0, nr)]

    own = piece(p, q, c)
    own[...] = w_own
    for o in OFFSETS:
        send(3, own, own, along_q(o))
    yield
    all_of(1, r1).wait_send()
    all_of(3, rq).wait_recv()
    own = group(p, c)
    come = [send(4, own, own, along_p(o), 4 + o) for o in OFFSETS]
    send(8, own, own, sibling)
    yield
    all_of(2, rq).wait_send()
    all_of(3, rq).wait_send()
    for i, o in ((1, 1), (2, 3), (0, 2)):
        come[i].wait_recv()
        got = group((p + 4 - o) % 4, c)
        send(8, got, got, sibling)
    yield
    all_of(4, r1).wait_send()
    all_of(8, s1).wait()
    yield


def kernel(
    tokens, key_cot, gain, key_weight, first_moment, second_moment, inner_step, global_prev, outer_momentum, replica_prev,
    weight_out, first_out, second_out, keys_out, blended_out, momentum_out,
    tok, cot, cs, scale, kw, m1, m2, gp, om, rp, gcol, wn, fn, sn, bl, mn, keys, w_all, ds, dy,
    step_smem, in_sem, out_sem, d_send, d_recv, *chunk_scratch,
):
    here = Place()
    c = here.c

    barrier = pltpu.get_barrier_semaphore()
    n_partners = 0
    for to in here.partners():
        pl.semaphore_signal(barrier, inc=1, device_id=to, device_id_type=MESH)
        n_partners += 1

    def load(src, dst, n):
        one = pltpu.make_async_copy(src, dst, in_sem.at[n])
        one.start()
        return one

    quarter = TOK // 4
    tok_in = [load(tokens.at[0, pl.ds(i * quarter, quarter)], tok.at[pl.ds(i * quarter, quarter)], i) for i in range(4)]
    cot_in = load(key_cot.at[0], cot, 4)
    rest = [
        load(key_weight.at[0], kw, 5),
        load(first_moment.at[0], m1, 6),
        load(second_moment.at[0], m2, 7),
        load(global_prev, gp, 8),
        load(outer_momentum, om, 9),
        load(inner_step, step_smem, 11),
    ]
    rp_in = load(replica_prev.at[0], rp, 10)

    for i in range(4):
        tok_in[i].wait()
        if i == 0:
            cot_in.wait()
        rows = slice(i * quarter, (i + 1) * quarter)
        v = up(tok[rows, :])
        s = lax.rsqrt(jnp.sum(v * v, axis=1, keepdims=True) * (1.0 / D) + 1e-05)
        scale[rows, :] = s
        cs[rows, :] = (up(cot[rows, :]) * s).astype(BF16)

    def gemm1(half):
        for x in range(4):
            part = lax.dot_general(
                tok[:, x * 512 : (x + 1) * 512],
                cs[:, half * WIDE : (half + 1) * WIDE],
                CONTRACT_FIRST,
                preferred_element_type=F32,
            ).astype(BF16)
            for i, (h, row0, nr, axis) in enumerate(CHUNKS):
                if h != half:
                    continue
                g = chunk_scratch[8 * i]
                for z in range(4):
                    p, q = (x, z) if axis == "x" else (z, x)
                    for cc in range(2):
                        at = (z * 2 + cc) * ROWS + row0
                        g[cc, p, q] = part[at : at + nr]

    def adam(half, row0, nr, total):
        rows, cols = slice(row0, row0 + nr), slice(half * WIDE, (half + 1) * WIDE)
        count = jnp.full((1, WIDE), step_smem[0], jnp.int32).astype(F32)
        gains = gcol[rows, :]
        grads = total * gains
        first_new = 0.9 * m1[rows, cols] + 0.1 * grads
        second_new = 0.95 * m2[rows, cols] + 0.05 * grads * grads
        first_hat = first_new / (1.0 - jnp.exp(count * math.log(0.9)))
        second_hat = second_new / (1.0 - jnp.exp(count * math.log(0.95)))
        weight = kw[rows, cols]
        change = 0.03 * (first_hat / (jnp.sqrt(second_hat) + 1e-08) + 0.1 * weight)
        weight_new = weight - change
        fn[rows, cols] = first_new
        sn[rows, cols] = second_new
        wn[rows, cols] = weight_new
        return (weight_new * gains).astype(BF16)

    outs = []

    def store(src, dst):
        one = pltpu.make_async_copy(src, dst, out_sem.at[len(outs)])
        one.start()
        outs.append(one)

    def drift_steps():
        y = here.y
        rp_in.wait()
        ds[0] = rp[...].astype(BF16)
        swap = remote(ds.at[0], ds.at[1], d_send.at[0], d_recv.at[0], here.at(l=1 - here.l))
        swap.start()
        yield
        swap.wait()
        dy[y] = (up(ds[0]) + up(ds[1])).astype(BF16)
        went = []
        for k in range(4):
            come = []
            for n, step in ((1 + k, 1), (5 + k, 7)):
                if k == 3 and step == 7:
                    continue
                slot = dy.at[(y + (8 - step) * k) % 8]
                one = remote(slot, slot, d_send.at[n], d_recv.at[n], here.at(y=(y + step) % 8))
                one.start()
                come.append(one)
            went += come
            yield
            for one in come:
                one.wait_recv()
        total = up(dy[0])
        for i in range(1, 8):
            total = total + up(dy[i])
        mean_drift = gp[...] - total * (1.0 / 16)
        momentum_new = 0.9 * om[...] + mean_drift
        global_new = gp[...] - 0.7 * (mean_drift + 0.9 * momentum_new)
        mn[...] = momentum_new
        bl[...] = 0.5 * global_new + 0.5 * rp[...]
        store(mn, momentum_out)
        store(bl, blended_out.at[0])
        for one in went:
            one.wait_send()
        yield

    def gemm2(half):
        w = w_all[half].reshape(D, WIDE)
        cols = slice(half * WIDE, (half + 1) * WIDE)
        part = jnp.dot(tok[...], w, preferred_element_type=F32)
        keys[half] = (part * scale[...]).astype(BF16)
        store(keys.at[half], keys_out.at[0, :, pl.ds(half * WIDE, WIDE)])

    chunks = [
        chunk_steps(here, chunk, chunk_scratch[8 * i : 8 * i + 6], chunk_scratch[8 * i + 6 : 8 * i + 8], w_all, adam)
        for i, chunk in enumerate(CHUNKS)
    ]
    drift = drift_steps()

    gemm1(HALVES[0])
    pl.semaphore_wait(barrier, n_partners)
    for i, chunk in enumerate(CHUNKS):
        if chunk[0] == HALVES[0]:
            next(chunks[i])
    next(drift)
    gemm1(HALVES[1])
    for i, chunk in enumerate(CHUNKS):
        if chunk[0] == HALVES[1]:
            next(chunks[i])
    for one in rest:
        one.wait()
    lane = lax.broadcasted_iota(jnp.int32, (ROWS, 128), 1)
    row = lax.broadcasted_iota(jnp.int32, (ROWS, 128), 0)
    gains = gain[pl.ds(here.x * 4 + here.z, 1), :]
    picked = jnp.where(lane == row + ROWS * c, jnp.broadcast_to(gains, (ROWS, 128)), 0.0)
    gcol[...] = jnp.broadcast_to(jnp.sum(picked, axis=1, keepdims=True), (ROWS, WIDE))

    for level in range(1, 6):
        for one in chunks:
            next(one)
        if level == 3:
            store(wn, weight_out.at[0])
            store(fn, first_out.at[0])
            store(sn, second_out.at[0])
        next(drift)
    for half in HALVES:
        for i, chunk in enumerate(CHUNKS):
            if chunk[0] == half:
                next(chunks[i])
        gemm2(half)
    for one in outs:
        one.wait()


def chunk_scratch(nr):
    return [
        pltpu.VMEM((2, 4, 4, nr, WIDE), BF16),
        pltpu.VMEM((4, 4, nr, WIDE), BF16),
        pltpu.VMEM((4, 4, nr, WIDE), BF16),
        pltpu.VMEM((3, 4, nr, WIDE), BF16),
        pltpu.VMEM((4, nr, WIDE), BF16),
        pltpu.VMEM((3, nr, WIDE), BF16),
        pltpu.SemaphoreType.DMA((9,)),
        pltpu.SemaphoreType.DMA((9,)),
    ]


def hand_over(*refs):
    given, wanted, held, sems = refs[:6], refs[6:12], refs[12:18], refs[18]
    come = [pltpu.make_async_copy(given[i], held[i], sems.at[0, i]) for i in range(6)]
    go = [pltpu.make_async_copy(held[i], wanted[i], sems.at[1, i]) for i in range(6)]
    for one in come:
        one.start()
    for i in range(6):
        come[i].wait()
        go[i].start()
    for one in go:
        one.wait()


def body(tokens, key_cot, norm_gain, key_weight, first_moment, second_moment, inner_step, global_prev, outer_momentum, replica_prev):
    anywhere = pl.BlockSpec(memory_space=pl.ANY)
    small = jax.ShapeDtypeStruct((1, ROWS, KW), F32)
    shard = pltpu.VMEM((ROWS, KW), F32)
    scratch = [
        pltpu.VMEM((TOK, D), BF16),
        pltpu.VMEM((TOK, KW), BF16),
        pltpu.VMEM((TOK, KW), BF16),
        pltpu.VMEM((TOK, 1), F32),
        *[shard] * 6,
        pltpu.VMEM((ROWS, WIDE), F32),
        *[shard] * 5,
        pltpu.VMEM((2, TOK, WIDE), BF16),
        pltpu.VMEM((2, 4, 4, 2, ROWS, WIDE), BF16),
        pltpu.VMEM((2, ROWS, KW), BF16),
        pltpu.VMEM((8, ROWS, KW), BF16),
        pltpu.SMEM((1,), jnp.int32),
        pltpu.SemaphoreType.DMA((12,)),
        pltpu.SemaphoreType.DMA((7,)),
        pltpu.SemaphoreType.DMA((8,)),
        pltpu.SemaphoreType.DMA((8,)),
    ]
    for chunk in CHUNKS:
        scratch += chunk_scratch(chunk[2])
    results = pl.pallas_call(
        kernel,
        out_shape=(
            small,
            small,
            small,
            jax.ShapeDtypeStruct((1, TOK, KW), BF16),
            small,
            jax.ShapeDtypeStruct((ROWS, KW), F32),
        ),
        in_specs=[
            anywhere,
            anywhere,
            pl.BlockSpec(memory_space=pltpu.VMEM),
            anywhere,
            anywhere,
            anywhere,
            anywhere,
            anywhere,
            anywhere,
            anywhere,
        ],
        out_specs=(anywhere,) * 6,
        scratch_shapes=scratch,
        name="step",
        compiler_params=pltpu.CompilerParams(
            collective_id=0, has_side_effects=True, vmem_limit_bytes=56 * 2**20
        ),
    )(
        tokens, key_cot, norm_gain.reshape(16, 128), key_weight, first_moment, second_moment, inner_step,
        global_prev, outer_momentum, replica_prev,
    )
    return pl.pallas_call(
        hand_over,
        out_shape=tuple(jax.ShapeDtypeStruct(a.shape, a.dtype) for a in results),
        in_specs=[anywhere] * 6,
        out_specs=(anywhere,) * 6,
        scratch_shapes=[*[pltpu.VMEM(a.shape, a.dtype) for a in results], pltpu.SemaphoreType.DMA((2, 6))],
        name="hand_over",
    )(*results)


def solution(mesh):
    split = P("replica", "fsdp", None)
    rows = P("fsdp", None)
    return jax.shard_map(
        body,
        mesh=mesh,
        in_specs=(split, split, P(), split, split, split, P(), rows, rows, split),
        out_specs=(split, split, split, split, split, rows),
        check_vma=False,
    )
```

time: 61.7 us -> 51.3 us (0.83)
  local copies, waits for them, and re-layouts: 8.83 us -> 0 us
  Pallas kernels: 51.3 us -> 49.4 us
    unnamed x8 -> x0, local copies, waits for them, and re-layouts: 8.83 us -> none
    pallas_call x1, Pallas kernels: 51.3 us -> 47.2 us  [body(): pl.pallas_call(kernel, out_shape=(small, small, small, jax.ShapeDtypeStru...]
    pallas_call x0 -> x1, Pallas kernels: none -> 2.22 us  [body(): pl.pallas_call(hand_over, out_shape=tuple((jax.ShapeDtypeStruct(a.shape,...]
where the time goes in v2:
time: 51.3 us; the launch traced here: 50.7 us
  Pallas kernels  49.4 us (96%)
  between operations  1.29 us (3%)
    pallas_call x1, Pallas kernels, body(): pl.pallas_call(kernel, out_shape=(small, small, small, jax.ShapeDtypeStru...  47.2 us
    pallas_call x1, Pallas kernels, body(): pl.pallas_call(hand_over, out_shape=tuple((jax.ShapeDtypeStruct(a.shape,...  2.22 us

profile of v2, /device:TPU:1, one launch (start us, length us, event | category | flops | bytes accessed | tf_op | source)
XLA Modules:
  0.0 50.7 jit_solution(16450954547310587440)
XLA Ops:
  1.3 47.2 %step.1 = (f32[1,64,512]{2,1,0:T(8,128)}, f32[1,64,512]{2,1,0:T(8,128)}, f32[1,64,512]{2,1,0:T(8,128)}, bf16[1,512,512]{2,1,0:T(8,128)(2,1)}, f32[1,64,512]{2,1,0:T(8,128)}, /*index=5*/f32[64,512]{1,0:T(8,128)}) custom-call(bf16[1,512,2048]{2,1,0:T(8,128)(2,1)} %tokens.1, bf16[1,512,512]{2,1,0:T(8,128)(2,1)} %key_cot.1, f32[16,128]{1,0:T(8,128)} %bitcast.1, ...), custom_call_target="tpu_custom_call" | custom-call | tf_op jit(solution)/shard_map/step/pallas_call | solution.py:353
  48.4 2.2 %hand_over.1 = (f32[1,64,512]{2,1,0:T(8,128)}, f32[1,64,512]{2,1,0:T(8,128)}, f32[1,64,512]{2,1,0:T(8,128)}, bf16[1,512,512]{2,1,0:T(8,128)(2,1)}, f32[1,64,512]{2,1,0:T(8,128)}, /*index=5*/f32[64,512]{1,0:T(8,128)}) custom-call(f32[1,64,512]{2,1,0:T(8,128)} %get-tuple-element.12.refs_0_, f32[1,64,512]{2,1,0:T(8,128)} %get-tuple-element.13.refs_1_, ...), custom_call_target="tpu_custom_call" | custom-call | tf_op jit(solution)/shard_map/hand_over/pallas_call | solution.py:385

commit v3 on v2

--- a/solution.py
+++ b/solution.py
@@ -12,12 +12,7 @@
 TOK, D, KW, ROWS, WIDE = 512, 2048, 512, 64, 256
 CONTRACT_FIRST = (((0,), (0,)), ((), ()))
 
-CHUNKS = (
-    (1, 32, 32, "z"),
-    (1, 0, 32, "x"),
-    (0, 0, 32, "x"),
-    (0, 32, 32, "x"),
-)
+CHUNKS = ((1, 32, 16, 'z'), (1, 0, 16, 'x'), (1, 48, 16, 'z'), (1, 16, 16, 'x'), (0, 0, 16, 'x'), (0, 16, 16, 'x'), (0, 32, 16, 'x'), (0, 48, 16, 'x'))
 HALVES = (1, 0)
 OFFSETS = (2, 1, 3)
 
@@ -133,8 +128,8 @@
 def kernel(
     tokens, key_cot, gain, key_weight, first_moment, second_moment, inner_step, global_prev, outer_momentum, replica_prev,
     weight_out, first_out, second_out, keys_out, blended_out, momentum_out,
-    tok, cot, cs, scale, kw, m1, m2, gp, om, rp, gcol, wn, fn, sn, bl, mn, keys, w_all, ds, dy,
-    step_smem, in_sem, out_sem, d_send, d_recv, *chunk_scratch,
+    tok, cot, cs, scale, kw, m1, m2, gp, om, rp, gcol, w_all, ds, dy,
+    step_smem, in_sem, d_send, d_recv, *chunk_scratch,
 ):
     here = Place()
     c = here.c
@@ -203,17 +198,10 @@
         weight = kw[rows, cols]
         change = 0.03 * (first_hat / (jnp.sqrt(second_hat) + 1e-08) + 0.1 * weight)
         weight_new = weight - change
-        fn[rows, cols] = first_new
-        sn[rows, cols] = second_new
-        wn[rows, cols] = weight_new
+        first_out[0, rows, cols] = first_new
+        second_out[0, rows, cols] = second_new
+        weight_out[0, rows, cols] = weight_new
         return (weight_new * gains).astype(BF16)
-
-    outs = []
-
-    def store(src, dst):
-        one = pltpu.make_async_copy(src, dst, out_sem.at[len(outs)])
-        one.start()
-        outs.append(one)
 
     def drift_steps():
         y = here.y
@@ -244,10 +232,8 @@
         mean_drift = gp[...] - total * (1.0 / 16)
         momentum_new = 0.9 * om[...] + mean_drift
         global_new = gp[...] - 0.7 * (mean_drift + 0.9 * momentum_new)
-        mn[...] = momentum_new
-        bl[...] = 0.5 * global_new + 0.5 * rp[...]
-        store(mn, momentum_out)
-        store(bl, blended_out.at[0])
+        momentum_out[...] = momentum_new
+        blended_out[0] = 0.5 * global_new + 0.5 * rp[...]
         for one in went:
             one.wait_send()
         yield
@@ -256,8 +242,7 @@
         w = w_all[half].reshape(D, WIDE)
         cols = slice(half * WIDE, (half + 1) * WIDE)
         part = jnp.dot(tok[...], w, preferred_element_type=F32)
-        keys[half] = (part * scale[...]).astype(BF16)
-        store(keys.at[half], keys_out.at[0, :, pl.ds(half * WIDE, WIDE)])
+        keys_out[0, :, cols] = (part * scale[...]).astype(BF16)
 
     chunks = [
         chunk_steps(here, chunk, chunk_scratch[8 * i : 8 * i + 6], chunk_scratch[8 * i + 6 : 8 * i + 8], w_all, adam)
@@ -286,18 +271,12 @@
     for level in range(1, 6):
         for one in chunks:
             next(one)
-        if level == 3:
-            store(wn, weight_out.at[0])
-            store(fn, first_out.at[0])
-            store(sn, second_out.at[0])
         next(drift)
     for half in HALVES:
         for i, chunk in enumerate(CHUNKS):
             if chunk[0] == half:
                 next(chunks[i])
         gemm2(half)
-    for one in outs:
-        one.wait()
 
 
 def chunk_scratch(nr):
@@ -314,21 +293,18 @@
 
 
 def hand_over(*refs):
-    given, wanted, held, sems = refs[:6], refs[6:12], refs[12:18], refs[18]
-    come = [pltpu.make_async_copy(given[i], held[i], sems.at[0, i]) for i in range(6)]
-    go = [pltpu.make_async_copy(held[i], wanted[i], sems.at[1, i]) for i in range(6)]
-    for one in come:
+    sems = refs[12]
+    copies = [pltpu.make_async_copy(refs[i], refs[6 + i], sems.at[i]) for i in range(6)]
+    for one in copies:
         one.start()
-    for i in range(6):
-        come[i].wait()
-        go[i].start()
-    for one in go:
+    for one in copies:
         one.wait()
 
 
 def body(tokens, key_cot, norm_gain, key_weight, first_moment, second_moment, inner_step, global_prev, outer_momentum, replica_prev):
     anywhere = pl.BlockSpec(memory_space=pl.ANY)
-    small = jax.ShapeDtypeStruct((1, ROWS, KW), F32)
+    in_hbm = pl.BlockSpec(memory_space=pltpu.HBM)
+    small = pltpu.VMEM((1, ROWS, KW), F32)
     shard = pltpu.VMEM((ROWS, KW), F32)
     scratch = [
         pltpu.VMEM((TOK, D), BF16),
@@ -337,14 +313,11 @@
         pltpu.VMEM((TOK, 1), F32),
         *[shard] * 6,
         pltpu.VMEM((ROWS, WIDE), F32),
-        *[shard] * 5,
-        pltpu.VMEM((2, TOK, WIDE), BF16),
         pltpu.VMEM((2, 4, 4, 2, ROWS, WIDE), BF16),
         pltpu.VMEM((2, ROWS, KW), BF16),
         pltpu.VMEM((8, ROWS, KW), BF16),
         pltpu.SMEM((1,), jnp.int32),
         pltpu.SemaphoreType.DMA((12,)),
-        pltpu.SemaphoreType.DMA((7,)),
         pltpu.SemaphoreType.DMA((8,)),
         pltpu.SemaphoreType.DMA((8,)),
     ]
@@ -356,27 +329,27 @@
             small,
             small,
             small,
-            jax.ShapeDtypeStruct((1, TOK, KW), BF16),
+            pltpu.VMEM((1, TOK, KW), BF16),
             small,
-            jax.ShapeDtypeStruct((ROWS, KW), F32),
+            pltpu.VMEM((ROWS, KW), F32),
         ),
         in_specs=[
-            anywhere,
-            anywhere,
+            in_hbm,
+            in_hbm,
             pl.BlockSpec(memory_space=pltpu.VMEM),
-            anywhere,
-            anywhere,
-            anywhere,
-            anywhere,
-            anywhere,
-            anywhere,
-            anywhere,
+            in_hbm,
+            in_hbm,
+            in_hbm,
+            in_hbm,
+            in_hbm,
+            in_hbm,
+            in_hbm,
         ],
-        out_specs=(anywhere,) * 6,
+        out_specs=(pl.BlockSpec(memory_space=pltpu.VMEM),) * 6,
         scratch_shapes=scratch,
         name="step",
         compiler_params=pltpu.CompilerParams(
-            collective_id=0, has_side_effects=True, vmem_limit_bytes=56 * 2**20
+            collective_id=0, has_side_effects=True, vmem_limit_bytes=55 * 2**20
         ),
     )(
         tokens, key_cot, norm_gain.reshape(16, 128), key_weight, first_moment, second_moment, inner_step,
@@ -385,10 +358,11 @@
     return pl.pallas_call(
         hand_over,
         out_shape=tuple(jax.ShapeDtypeStruct(a.shape, a.dtype) for a in results),
-        in_specs=[anywhere] * 6,
-        out_specs=(anywhere,) * 6,
-        scratch_shapes=[*[pltpu.VMEM(a.shape, a.dtype) for a in results], pltpu.SemaphoreType.DMA((2, 6))],
+        in_specs=[pl.BlockSpec(memory_space=pltpu.VMEM)] * 6,
+        out_specs=(pl.BlockSpec(memory_space=pltpu.HBM),) * 6,
+        scratch_shapes=[pltpu.SemaphoreType.DMA((6,))],
         name="hand_over",
+        compiler_params=pltpu.CompilerParams(vmem_limit_bytes=4 * 2**20),
     )(*results)
 
 

time: 51.3 us -> 48.4 us (0.943)
  Pallas kernels: 49.4 us -> 46.9 us
    pallas_call x1, Pallas kernels: 47.2 us -> 45.8 us  [body(): pl.pallas_call(kernel, out_shape=(small, small, small, pltpu.VMEM((1, TOK...]
    pallas_call x1, Pallas kernels: 2.22 us -> 1.06 us  [body(): pl.pallas_call(hand_over, out_shape=tuple((jax.ShapeDtypeStruct(a.shape,...]
where the time goes in v3:
time: 48.4 us; the launch traced here: 48.2 us
  Pallas kernels  46.9 us (97%)
  between operations  1.29 us (3%)
    pallas_call x1, Pallas kernels, body(): pl.pallas_call(kernel, out_shape=(small, small, small, pltpu.VMEM((1, TOK...  45.8 us
    pallas_call x1, Pallas kernels, body(): pl.pallas_call(hand_over, out_shape=tuple((jax.ShapeDtypeStruct(a.shape,...  1.06 us

profile of v3, /device:TPU:1, one launch (start us, length us, event | category | flops | bytes accessed | tf_op | source)
XLA Modules:
  0.0 48.2 jit_solution(9072709047960281013)
XLA Ops:
  1.3 45.8 %step.1 = (f32[1,64,512]{2,1,0:T(8,128)S(1)}, f32[1,64,512]{2,1,0:T(8,128)S(1)}, f32[1,64,512]{2,1,0:T(8,128)S(1)}, bf16[1,512,512]{2,1,0:T(8,128)(2,1)S(1)}, f3...) custom-call(bf16[1,512,2048]{2,1,0:T(8,128)(2,1)} %tokens.1, bf16[1,512,512]{2,1,0:T(8,128)(2,1)} %key_cot.1, ...), custom_call_target="tpu_custom_call" | custom-call | tf_op jit(solution)/shard_map/step/pallas_call | solution.py:326
  47.1 1.1 %hand_over.1 = (f32[1,64,512]{2,1,0:T(8,128)}, f32[1,64,512]{2,1,0:T(8,128)}, f32[1,64,512]{2,1,0:T(8,128)}, bf16[1,512,512]{2,1,0:T(8,128)(2,1)}, f32[1,64,512]{2,1,0:T(8,128)}, /*index=5*/f32[64,512]{1,0:T(8,128)}) custom-call(f32[1,64,512]{2,1,0:T(8,128)S(1)} %get-tuple-element.12.refs_0_, f32[1,64,512]{2,1,0:T(8,128)S(1)} %get-tuple-element.13.refs_1_, ...), custom_call_target="tpu_custom_call" | custom-call | tf_op jit(solution)/shard_map/hand_over/pallas_call | solution.py:358

commit v4 on v3

--- a/solution.py
+++ b/solution.py
@@ -12,7 +12,16 @@
 TOK, D, KW, ROWS, WIDE = 512, 2048, 512, 64, 256
 CONTRACT_FIRST = (((0,), (0,)), ((), ()))
 
-CHUNKS = ((1, 32, 16, 'z'), (1, 0, 16, 'x'), (1, 48, 16, 'z'), (1, 16, 16, 'x'), (0, 0, 16, 'x'), (0, 16, 16, 'x'), (0, 32, 16, 'x'), (0, 48, 16, 'x'))
+CHUNKS = (
+    (1, 32, 16, "x"),
+    (1, 0, 16, "x"),
+    (1, 48, 16, "z"),
+    (1, 16, 16, "x"),
+    (0, 0, 16, "z"),
+    (0, 16, 16, "x"),
+    (0, 32, 16, "x"),
+    (0, 48, 16, "x"),
+)
 HALVES = (1, 0)
 OFFSETS = (2, 1, 3)
 
@@ -134,20 +143,20 @@
     here = Place()
     c = here.c
 
+    def load(src, dst, n):
+        one = pltpu.make_async_copy(src, dst, in_sem.at[n])
+        one.start()
+        return one
+
+    quarter = TOK // 4
+    tok_in = [load(tokens.at[0, pl.ds(i * quarter, quarter)], tok.at[pl.ds(i * quarter, quarter)], i) for i in range(4)]
+    cot_in = load(key_cot.at[0], cot, 4)
     barrier = pltpu.get_barrier_semaphore()
     n_partners = 0
     for to in here.partners():
         pl.semaphore_signal(barrier, inc=1, device_id=to, device_id_type=MESH)
         n_partners += 1
 
-    def load(src, dst, n):
-        one = pltpu.make_async_copy(src, dst, in_sem.at[n])
-        one.start()
-        return one
-
-    quarter = TOK // 4
-    tok_in = [load(tokens.at[0, pl.ds(i * quarter, quarter)], tok.at[pl.ds(i * quarter, quarter)], i) for i in range(4)]
-    cot_in = load(key_cot.at[0], cot, 4)
     rest = [
         load(key_weight.at[0], kw, 5),
         load(first_moment.at[0], m1, 6),

time: 48.4 us -> 47.3 us (0.977)
  Pallas kernels: 46.9 us -> 45.8 us
    pallas_call x1, Pallas kernels: 45.8 us -> 44.8 us  [body(): pl.pallas_call(kernel, out_shape=(small, small, small, pltpu.VMEM((1, TOK...]
where the time goes in v4:
time: 47.3 us; the launch traced here: 47.1 us
  Pallas kernels  45.8 us (97%)
  between operations  1.29 us (3%)
    pallas_call x1, Pallas kernels, body(): pl.pallas_call(kernel, out_shape=(small, small, small, pltpu.VMEM((1, TOK...  44.8 us
    pallas_call x1, Pallas kernels, body(): pl.pallas_call(hand_over, out_shape=tuple((jax.ShapeDtypeStruct(a.shape,...  1.06 us

profile of v4, /device:TPU:1, one launch (start us, length us, event | category | flops | bytes accessed | tf_op | source)
XLA Modules:
  0.0 47.1 jit_solution(897146216387910960)
XLA Ops:
  1.3 44.8 %step.1 = (f32[1,64,512]{2,1,0:T(8,128)S(1)}, f32[1,64,512]{2,1,0:T(8,128)S(1)}, f32[1,64,512]{2,1,0:T(8,128)S(1)}, bf16[1,512,512]{2,1,0:T(8,128)(2,1)S(1)}, f3...) custom-call(bf16[1,512,2048]{2,1,0:T(8,128)(2,1)} %tokens.1, bf16[1,512,512]{2,1,0:T(8,128)(2,1)} %key_cot.1, ...), custom_call_target="tpu_custom_call" | custom-call | tf_op jit(solution)/shard_map/step/pallas_call | solution.py:335
  46.0 1.1 %hand_over.1 = (f32[1,64,512]{2,1,0:T(8,128)}, f32[1,64,512]{2,1,0:T(8,128)}, f32[1,64,512]{2,1,0:T(8,128)}, bf16[1,512,512]{2,1,0:T(8,128)(2,1)}, f32[1,64,512]{2,1,0:T(8,128)}, /*index=5*/f32[64,512]{1,0:T(8,128)}) custom-call(f32[1,64,512]{2,1,0:T(8,128)S(1)} %get-tuple-element.12.refs_0_, f32[1,64,512]{2,1,0:T(8,128)S(1)} %get-tuple-element.13.refs_1_, ...), custom_call_target="tpu_custom_call" | custom-call | tf_op jit(solution)/shard_map/hand_over/pallas_call | solution.py:367

commit v5 on v4

--- a/solution.py
+++ b/solution.py
@@ -64,6 +64,7 @@
 
 def chunk_steps(here, chunk, bufs, sems, w_ref, adam):
     half, row0, nr, axis = chunk
+    offsets = OFFSETS if row0 % 32 == 0 else (2, 3, 1)
     g, rc, s1, r1, sq, rq = bufs
     send_sem, recv_sem = sems
     other_axis = "z" if axis == "x" else "x"
@@ -87,7 +88,7 @@
     swap = send(0, g.at[1 - c], rc, sibling)
     yield
     swap.wait_recv()
-    for o in OFFSETS:
+    for o in offsets:
         to = (p + o) % 4
         s1[to] = (up(g[c, to]) + up(rc[to])).astype(BF16)
         send(1, s1.at[to], r1.at[o - 1], along_p(o))
@@ -95,7 +96,7 @@
     mine = up(g[c, p]) + up(rc[p])
     all_of(1, r1).wait_recv()
     sq[...] = (mine + up(r1[0]) + up(r1[1]) + up(r1[2])).astype(BF16)
-    for o in OFFSETS:
+    for o in offsets:
         send(2, sq.at[(q + o) % 4], rq.at[o - 1], along_q(o))
     yield
     swap.wait_send()
@@ -113,19 +114,19 @@
 
     own = piece(p, q, c)
     own[...] = w_own
-    for o in OFFSETS:
+    for o in offsets:
         send(3, own, own, along_q(o))
     yield
     all_of(1, r1).wait_send()
     all_of(3, rq).wait_recv()
     own = group(p, c)
-    come = [send(4, own, own, along_p(o), 4 + o) for o in OFFSETS]
+    come = [send(4, own, own, along_p(o), 4 + o) for o in offsets]
     send(8, own, own, sibling)
     yield
     all_of(2, rq).wait_send()
     all_of(3, rq).wait_send()
-    for i, o in ((1, 1), (2, 3), (0, 2)):
-        come[i].wait_recv()
+    for o in (1, 3, 2):
+        come[offsets.index(o)].wait_recv()
         got = group((p + 4 - o) % 4, c)
         send(8, got, got, sibling)
     yield

time: 47.3 us -> 47.3 us (level)
  no operation moved by 1% of the time
where the time goes in v5:
time: 47.3 us; the launch traced here: 47.1 us
  Pallas kernels  45.8 us (97%)
  between operations  1.29 us (3%)
    pallas_call x1, Pallas kernels, body(): pl.pallas_call(kernel, out_shape=(small, small, small, pltpu.VMEM((1, TOK...  44.8 us
    pallas_call x1, Pallas kernels, body(): pl.pallas_call(hand_over, out_shape=tuple((jax.ShapeDtypeStruct(a.shape,...  1.06 us

profile of v5, /device:TPU:1, one launch (start us, length us, event | category | flops | bytes accessed | tf_op | source)
XLA Modules:
  0.0 47.1 jit_solution(15665081813123371647)
XLA Ops:
  1.3 44.8 %step.1 = (f32[1,64,512]{2,1,0:T(8,128)S(1)}, f32[1,64,512]{2,1,0:T(8,128)S(1)}, f32[1,64,512]{2,1,0:T(8,128)S(1)}, bf16[1,512,512]{2,1,0:T(8,128)(2,1)S(1)}, f3...) custom-call(bf16[1,512,2048]{2,1,0:T(8,128)(2,1)} %tokens.1, bf16[1,512,512]{2,1,0:T(8,128)(2,1)} %key_cot.1, ...), custom_call_target="tpu_custom_call" | custom-call | tf_op jit(solution)/shard_map/step/pallas_call | solution.py:336
  46.0 1.1 %hand_over.1 = (f32[1,64,512]{2,1,0:T(8,128)}, f32[1,64,512]{2,1,0:T(8,128)}, f32[1,64,512]{2,1,0:T(8,128)}, bf16[1,512,512]{2,1,0:T(8,128)(2,1)}, f32[1,64,512]{2,1,0:T(8,128)}, /*index=5*/f32[64,512]{1,0:T(8,128)}) custom-call(f32[1,64,512]{2,1,0:T(8,128)S(1)} %get-tuple-element.12.refs_0_, f32[1,64,512]{2,1,0:T(8,128)S(1)} %get-tuple-element.13.refs_1_, ...), custom_call_target="tpu_custom_call" | custom-call | tf_op jit(solution)/shard_map/hand_over/pallas_call | solution.py:368
